TPU v7x, 512 devices: a whole 4x4x16 slice. The times are simulated.
512 devices in a mesh: leaf: 64 (over z, y), sec: 8 (over x, core).
Axes of the slice: x: 4, y: 4, z: 16, core: 2. Of those that a mesh axis runs over, the one named last changes fastest.
Arguments:
- leaf_inv: bfloat16 [524288, 1024], P(('leaf', 'sec')), may hold values from -0.1875 to 0.1875
- subtree_blocks: int32 [64, 8], P('leaf', 'sec'), may hold values from 1 to 8
- subtree_shift_rhs: bfloat16 [524288, 128], P(('leaf', 'sec')), may hold values from -6 to 6
- leaf_noise: bfloat16 [524288, 128], P(('leaf', 'sec')), may hold values from -6 to 6
- leaf_dev: bfloat16 [524288], P(('leaf', 'sec')), may hold values from 0.29882812 to 3
- sep_inv: bfloat16 [16384, 3584], P(('leaf', 'sec')), may hold values from -0.1875 to 0.1875
- sep_panel: bfloat16 [16384, 3584], P(('leaf', 'sec')), may hold values from -0.1875 to 0.1875
- sep_rhs: bfloat16 [3, 16384, 128], P(None, ('leaf', 'sec')), may hold values from -6 to 6
- sep_noise: bfloat16 [3, 16384, 128], P(None, ('leaf', 'sec')), may hold values from -6 to 6
- sep_dev: bfloat16 [3, 16384], P(None, ('leaf', 'sec')), may hold values from 0.29882812 to 3
Outputs:
- subtree_scaled_samples: bfloat16 [524288, 128], P(('leaf', 'sec'))
- sep_sample: bfloat16 [3, 16384, 128], P(None, ('leaf', 'sec'))
All inputs are finite; a program needn't handle non-finite values.
Results may differ from a plain program's by a relative error of at most 0.019.
Values may be sent and summed in bfloat16 or wider, within the bound.
A program may use at most 64 MiB of HBM per device.

v0:
```python
import jax
import jax.numpy as jnp
from jax import lax
from jax.sharding import PartitionSpec as P

BLOCK = 128


def from_partner(block, axis, apart):
    count = lax.axis_size(axis)
    route = []
    for low in range(count):
        high = low | 1 << apart
        if high != low and high < count:
            route += [(low, high), (high, low)]
    return lax.ppermute(block, axis, route)


def pair_gather(block, height):
    leaf_place = lax.axis_index("leaf")
    for bit_index in range(height):
        partner = from_partner(block, "leaf", bit_index)
        upper_half = leaf_place >> bit_index & 1 == 1
        block = jnp.where(
            upper_half, jnp.concatenate([partner, block], 0), jnp.concatenate([block, partner], 0)
        )
    return block


def group_gather(piece, height):
    block = lax.all_gather(piece, "sec", axis=0, tiled=True)
    return pair_gather(block, height)


def halve_pairs(partial_sum, height):
    leaf_place = lax.axis_index("leaf")
    for bit_index in reversed(range(height)):
        half_rows = partial_sum.shape[0] // 2
        lower_rows = partial_sum[:half_rows]
        upper_rows = partial_sum[half_rows:]
        upper_half = leaf_place >> bit_index & 1 == 1
        kept = jnp.where(upper_half, upper_rows, lower_rows)
        outgoing = jnp.where(upper_half, lower_rows, upper_rows)
        partial_sum = kept + from_partner(outgoing, "leaf", bit_index)
    return partial_sum


def group_reduce(partial_sum, height):
    reduced = halve_pairs(partial_sum, height)
    return lax.psum_scatter(reduced, "sec", scatter_dimension=0, tiled=True)


def transposed_product(matrix, vector):
    return lax.dot_general(
        matrix, vector, (((0,), (0,)), ((), ())), preferred_element_type=jnp.float32
    )


def on_device(
    leaf_inv,
    subtree_blocks,
    subtree_shift_rhs,
    leaf_noise,
    leaf_dev,
    sep_inv,
    sep_panel,
    sep_rhs,
    sep_noise,
    sep_dev,
):
    subtree_row_count = leaf_inv.shape[0]
    row_count = sep_inv.shape[0]
    levels = sep_rhs.shape[0]
    sections = lax.axis_size("sec")
    active_rows = subtree_blocks[0, 0] * BLOCK
    row_positions = jnp.arange(subtree_row_count, dtype=jnp.int32)
    row_activity = (row_positions >= subtree_row_count - active_rows)[:, None]
    subtree_shifted = jnp.where(
        row_activity, subtree_shift_rhs, jnp.zeros((), subtree_shift_rhs.dtype)
    )
    forward_subtree = jnp.dot(leaf_inv, subtree_shifted, preferred_element_type=jnp.float32)
    subtree_forward_solution = jnp.where(row_activity, forward_subtree, jnp.float32(0.0)).astype(
        jnp.bfloat16
    )
    top = subtree_forward_solution[subtree_row_count - row_count :]
    solved = []
    for height in range(1, levels + 1):
        span = 2**height * sections * row_count
        offset = (2**height - 2) * sections * row_count
        children = group_gather(top, height)
        panel = sep_panel[:, offset : offset + span]
        inverse_block = sep_inv[:, offset : offset + span]
        reduced = (
            sep_rhs[height - 1].astype(jnp.float32)
            - jnp.dot(panel, children, preferred_element_type=jnp.float32)
        ).astype(jnp.bfloat16)
        whole_reduced = group_gather(reduced, height)
        result = jnp.dot(inverse_block, whole_reduced, preferred_element_type=jnp.float32).astype(
            jnp.bfloat16
        )
        solved.append(result)
        top = result
    samples = [None] * levels
    correction = None
    for height in range(levels, 0, -1):
        span = 2**height * sections * row_count
        offset = (2**height - 2) * sections * row_count
        panel = sep_panel[:, offset : offset + span]
        inverse_block = sep_inv[:, offset : offset + span]
        summed = solved[height - 1].astype(jnp.float32) + sep_noise[height - 1].astype(jnp.float32)
        if correction is not None:
            summed = summed - correction
        vector = summed.astype(jnp.bfloat16)
        backed = group_reduce(transposed_product(inverse_block, vector), height).astype(
            jnp.bfloat16
        )
        samples[height - 1] = (
            sep_dev[height - 1][:, None].astype(jnp.float32) * backed.astype(jnp.float32)
        ).astype(jnp.bfloat16)
        correction = group_reduce(transposed_product(panel, backed), height)
    leading = jnp.zeros((subtree_row_count - row_count, correction.shape[1]), jnp.float32)
    placed = jnp.concatenate([leading, correction], axis=0)
    subtree_summed = (
        subtree_forward_solution.astype(jnp.float32) + leaf_noise.astype(jnp.float32) - placed
    )
    subtree_weight = jnp.where(row_activity, subtree_summed, jnp.float32(0.0)).astype(jnp.bfloat16)
    subtree_solution = transposed_product(leaf_inv, subtree_weight)
    sample_scales = leaf_dev[:, None].astype(jnp.float32)
    subtree_scaled_samples = jnp.where(
        row_activity, sample_scales * subtree_solution, jnp.float32(0.0)
    ).astype(jnp.bfloat16)
    return (subtree_scaled_samples, jnp.stack(samples))


def solution(mesh):
    in_specs = (
        P(("leaf", "sec"), None),
        P("leaf", "sec"),
        P(("leaf", "sec"), None),
        P(("leaf", "sec"), None),
        P(("leaf", "sec")),
        P(("leaf", "sec"), None),
        P(("leaf", "sec"), None),
        P(None, ("leaf", "sec"), None),
        P(None, ("leaf", "sec"), None),
        P(None, ("leaf", "sec")),
    )
    out_specs = (P(("leaf", "sec"), None), P(None, ("leaf", "sec"), None))
    return jax.shard_map(
        on_device, mesh=mesh, in_specs=in_specs, out_specs=out_specs, check_vma=False
    )
```

profile of v0, /device:TPU:8, one launch (start us, length us, event | category | flops | bytes accessed | tf_op | source)
XLA Modules:
  0.0 543.7 jit_solution(11738488947053809435)
XLA Ops:
  10.1 13.1 %all_gather.18 = bf16[256,128]{1,0:T(8,128)(2,1)S(1)} all-gather(bf16[32,128]{1,0:T(8,128)(2,1)S(1)} %copy.28), channel_id=1, replica_groups=mesh['leaf'=64,'sec'=8] {'sec'}, dimensions={0}, use_global_device_ids=true | all-gather | bytes 73728 | tf_op jit(solution)/shard_map/all_gather | solution.py:31
  23.3 7.4 %collective-permute-start = (bf16[256,128]{1,0:T(8,128)(2,1)S(1)}, bf16[256,128]{1,0:T(8,128)(2,1)S(1)}, u32[]{:S(2)}, u32[]{:S(2)}) collective-permute-start(bf16[256,128]{1,0:T(8,128)(2,1)S(1)} %all_gather.18), channel_id=1, source_target_pairs={{0,8},{8,0},{16,24},{24,16},{32,40},{40,32},{48,56},{56,48},{64,72... | collective-permute-start | bytes 196616 | tf_op jit(solution)/shard_map/ppermute | solution.py:16
  33.3 12.7 %all_gather.19 = bf16[256,128]{1,0:T(8,128)(2,1)S(1)} all-gather(bf16[32,128]{1,0:T(8,128)(2,1)S(1)} %fusion.8), channel_id=1, replica_groups=mesh['leaf'=64,'sec'=8] {'sec'}, dimensions={0}, use_global_device_ids=true | all-gather | bytes 73728 | tf_op jit(solution)/shard_map/all_gather | solution.py:31
  46.1 3.6 collective-permute-start.1
  49.7 2.6 collective-permute-done.1
  53.2 12.7 %all_gather.20 = bf16[256,128]{1,0:T(8,128)(2,1)S(1)} all-gather(bf16[32,128]{1,0:T(8,128)(2,1)S(1)} %fusion.15), channel_id=1, replica_groups=mesh['leaf'=64,'sec'=8] {'sec'}, dimensions={0}, use_global_device_ids=true | all-gather | bytes 73728 | tf_op jit(solution)/shard_map/all_gather | solution.py:31
  65.9 3.6 collective-permute-start.2
  69.6 2.6 collective-permute-done.2
  74.1 6.4 %collective-permute-done.3 = bf16[512,128]{1,0:T(8,128)(2,1)S(1)} collective-permute-done((bf16[512,128]{1,0:T(8,128)(2,1)S(1)}, bf16[512,128]{1,0:T(8,128)(2,1)S(1)}, u32[]{:S(2)}, u32[]{:S(2)}) %collective-permute-start.3) | collective-permute-done | bytes 131104 | tf_op jit(solution)/shard_map/ppermute | solution.py:16
  80.7 12.8 %all_gather.21 = bf16[256,128]{1,0:T(8,128)(2,1)S(1)} all-gather(bf16[32,128]{1,0:T(8,128)(2,1)S(1)} %fusion.9), channel_id=1, replica_groups=mesh['leaf'=64,'sec'=8] {'sec'}, dimensions={0}, use_global_device_ids=true | all-gather | bytes 73728 | tf_op jit(solution)/shard_map/all_gather | solution.py:31
  93.5 3.6 collective-permute-start.4
  97.1 2.6 collective-permute-done.4
  101.9 6.2 %collective-permute-done.5 = bf16[512,128]{1,0:T(8,128)(2,1)S(1)} collective-permute-done((bf16[512,128]{1,0:T(8,128)(2,1)S(1)}, bf16[512,128]{1,0:T(8,128)(2,1)S(1)}, u32[]{:S(2)}, u32[]{:S(2)}) %collective-permute-start.5) | collective-permute-done | bytes 131104 | tf_op jit(solution)/shard_map/ppermute | solution.py:16
  109.1 12.8 %all_gather.22 = bf16[256,128]{1,0:T(8,128)(2,1)S(1)} all-gather(bf16[32,128]{1,0:T(8,128)(2,1)S(1)} %fusion.16), channel_id=1, replica_groups=mesh['leaf'=64,'sec'=8] {'sec'}, dimensions={0}, use_global_device_ids=true | all-gather | bytes 73728 | tf_op jit(solution)/shard_map/all_gather | solution.py:31
  121.9 3.6 collective-permute-start.6
  130.3 6.2 %collective-permute-done.7 = bf16[512,128]{1,0:T(8,128)(2,1)S(1)} collective-permute-done((bf16[512,128]{1,0:T(8,128)(2,1)S(1)}, bf16[512,128]{1,0:T(8,128)(2,1)S(1)}, u32[]{:S(2)}, u32[]{:S(2)}) %collective-permute-start.7) | collective-permute-done | bytes 131104 | tf_op jit(solution)/shard_map/ppermute | solution.py:16
  138.5 6.5 %collective-permute-done.8 = bf16[1024,128]{1,0:T(8,128)(2,1)S(1)} collective-permute-done((bf16[1024,128]{1,0:T(8,128)(2,1)S(1)}, bf16[1024,128]{1,0:T(8,128)(2,1)S(1)}, u32[]{:S(2)}, u32[]{:S(2)}) %collective-permute-start.8) | collective-permute-done | bytes 262176 | tf_op jit(solution)/shard_map/ppermute | solution.py:16
  145.3 12.8 %all_gather.23 = bf16[256,128]{1,0:T(8,128)(2,1)S(1)} all-gather(bf16[32,128]{1,0:T(8,128)(2,1)S(1)} %fusion.10), channel_id=1, replica_groups=mesh['leaf'=64,'sec'=8] {'sec'}, dimensions={0}, use_global_device_ids=true | all-gather | bytes 73728 | tf_op jit(solution)/shard_map/all_gather | solution.py:31
  158.0 3.6 collective-permute-start.9
  161.7 2.6 collective-permute-done.9
  166.5 6.2 %collective-permute-done.10 = bf16[512,128]{1,0:T(8,128)(2,1)S(1)} collective-permute-done((bf16[512,128]{1,0:T(8,128)(2,1)S(1)}, bf16[512,128]{1,0:T(8,128)(2,1)S(1)}, u32[]{:S(2)}, u32[]{:S(2)}) %collective-permute-start.10) | collective-permute-done | bytes 131104 | tf_op jit(solution)/shard_map/ppermute | solution.py:16
  175.0 6.4 %collective-permute-done.11 = bf16[1024,128]{1,0:T(8,128)(2,1)} collective-permute-done((bf16[1024,128]{1,0:T(8,128)(2,1)S(1)}, bf16[1024,128]{1,0:T(8,128)(2,1)}, u32[]{:S(2)}, u32[]{:S(2)}) %collective-permute-start.11) | collective-permute-done | bytes 262176 | tf_op jit(solution)/shard_map/ppermute | solution.py:16
  185.5 11.0 %collective-permute-done.12 = f32[1024,128]{0,1:T(8,128)S(1)} collective-permute-done((f32[1024,128]{0,1:T(8,128)S(1)}, f32[1024,128]{0,1:T(8,128)S(1)}, u32[]{:S(2)}, u32[]{:S(2)}) %collective-permute-start.12) | collective-permute-done | bytes 524320 | tf_op jit(solution)/shard_map/ppermute | solution.py:16
  198.9 8.2 %collective-permute-done.13 = f32[512,128]{0,1:T(8,128)S(1)} collective-permute-done((f32[512,128]{0,1:T(8,128)S(1)}, f32[512,128]{0,1:T(8,128)S(1)}, u32[]{:S(2)}, u32[]{:S(2)}) %collective-permute-start.13) | collective-permute-done | bytes 262176 | tf_op jit(solution)/shard_map/ppermute | solution.py:16
  207.2 3.9 collective-permute-start.14
  211.0 3.0 collective-permute-done.14
  214.9 37.6 %reduce-scatter.19.cloned.1.call-done = f32[32,128]{1,0:T(8,128)} async-done(((f32[256,128]{1,0:T(8,128)}), f32[32,128]{1,0:T(8,128)}) %reduce-scatter.19.cloned.1.call-update) | async-done | bytes 16400
  253.7 3.6 collective-permute-start.15
  257.3 9.5 %collective-permute-done.15 = f32[1024,128]{0,1:T(8,128)S(1)} collective-permute-done((f32[1024,128]{0,1:T(8,128)S(1)}, f32[1024,128]{0,1:T(8,128)S(1)}, u32[]{:S(2)}, u32[]{:S(2)}) %collective-permute-start.15) | collective-permute-done | bytes 524320 | tf_op jit(solution)/shard_map/ppermute | solution.py:16
  266.9 4.1 collective-permute-start.16
  271.0 5.7 %collective-permute-done.16 = f32[512,128]{0,1:T(8,128)S(1)} collective-permute-done((f32[512,128]{0,1:T(8,128)S(1)}, f32[512,128]{0,1:T(8,128)S(1)}, u32[]{:S(2)}, u32[]{:S(2)}) %collective-permute-start.16) | collective-permute-done | bytes 262176 | tf_op jit(solution)/shard_map/ppermute | solution.py:16
  276.7 3.5 collective-permute-start.17
  280.3 3.3 collective-permute-done.17
  284.5 41.8 %reduce-scatter.21.cloned.1.call-done = f32[32,128]{1,0:T(8,128)} async-done(((f32[256,128]{1,0:T(8,128)}), f32[32,128]{1,0:T(8,128)}) %reduce-scatter.21.cloned.1.call-update) | async-done | bytes 16400 | tf_op jit(solution)/shard_map/reduce_scatter | solution.py:50
  327.4 4.0 collective-permute-start.18
  331.4 5.8 %collective-permute-done.18 = f32[512,128]{0,1:T(8,128)S(1)} collective-permute-done((f32[512,128]{0,1:T(8,128)S(1)}, f32[512,128]{0,1:T(8,128)S(1)}, u32[]{:S(2)}, u32[]{:S(2)}) %collective-permute-start.18) | collective-permute-done | bytes 262176 | tf_op jit(solution)/shard_map/ppermute | solution.py:16
  337.2 2.6 collective-permute-start.19
  339.8 4.3 collective-permute-done.19
  344.9 39.3 %reduce-scatter.23.cloned.1.call-done = f32[32,128]{1,0:T(8,128)} async-done(((f32[256,128]{1,0:T(8,128)}), f32[32,128]{1,0:T(8,128)}) %reduce-scatter.23.cloned.1.call-update) | async-done | bytes 16400
  385.4 4.2 collective-permute-start.20
  389.6 5.7 %collective-permute-done.20 = f32[512,128]{0,1:T(8,128)S(1)} collective-permute-done((f32[512,128]{0,1:T(8,128)S(1)}, f32[512,128]{0,1:T(8,128)S(1)}, u32[]{:S(2)}, u32[]{:S(2)}) %collective-permute-start.20) | collective-permute-done | bytes 262176 | tf_op jit(solution)/shard_map/ppermute | solution.py:16
  395.4 2.6 collective-permute-start.21
  397.9 4.3 collective-permute-done.21
  403.1 39.4 %reduce-scatter.25.cloned.1.call-done = f32[32,128]{1,0:T(8,128)} async-done(((f32[256,128]{1,0:T(8,128)}), f32[32,128]{1,0:T(8,128)}) %reduce-scatter.25.cloned.1.call-update) | async-done | bytes 16400 | tf_op jit(solution)/shard_map/reduce_scatter | solution.py:50
  446.0 4.4 collective-permute-done.22
  451.5 37.2 %reduce-scatter.27.cloned.1.call-done = f32[32,128]{1,0:T(8,128)} async-done(((f32[256,128]{1,0:T(8,128)}), f32[32,128]{1,0:T(8,128)}) %reduce-scatter.27.cloned.1.call-update) | async-done | bytes 16400
  492.3 4.3 collective-permute-done.23
  498.1 36.7 %reduce-scatter.29.cloned.1.call-done = f32[32,128]{1,0:T(8,128)} async-done(((f32[256,128]{1,0:T(8,128)}), f32[32,128]{1,0:T(8,128)}) %reduce-scatter.29.cloned.1.call-update) | async-done | bytes 16400
  (110 shorter events, 48.0 us)
Async XLA Ops:
  7.2 2.0 copy-start
  7.2 26.0 %copy-start.3 = (bf16[32,3584]{1,0:T(8,128)(2,1)S(1)}, bf16[32,3584]{1,0:T(8,128)(2,1)}, u32[]{:S(2)}) copy-start(bf16[32,3584]{1,0:T(8,128)(2,1)} %param.16) | copy-start | bytes 688132
  7.2 26.0 %copy-start.8 = (bf16[3,32,128]{2,1,0:T(8,128)(2,1)S(1)}, bf16[3,32,128]{2,1,0:T(8,128)(2,1)}, u32[]{:S(2)}) copy-start(bf16[3,32,128]{2,1,0:T(8,128)(2,1)} %param.17) | copy-start | bytes 73732
  7.2 245.3 %reduce-scatter.19.cloned.1.call-start = ((), (), s32[]{:S(2)}) async-start(), calls=%async_computation.6 | async-start | bytes 147456
  23.3 9.9 %collective-permute-start = (bf16[256,128]{1,0:T(8,128)(2,1)S(1)}, bf16[256,128]{1,0:T(8,128)(2,1)S(1)}, u32[]{:S(2)}, u32[]{:S(2)}) collective-permute-start(bf16[256,128]{1,0:T(8,128)(2,1)S(1)} %all_gather.18), channel_id=1, source_target_pairs={{0,8},{8,0},{16,24},{24,16},{32,40},{40,32},{48,56},{56,48},{64,72... | collective-permute-start | bytes 196616 | tf_op jit(solution)/shard_map/ppermute | solution.py:16
  46.1 6.2 %collective-permute-start.1 = (bf16[256,128]{1,0:T(8,128)(2,1)S(1)}, bf16[256,128]{1,0:T(8,128)(2,1)S(1)}, u32[]{:S(2)}, u32[]{:S(2)}) collective-permute-start(bf16[256,128]{1,0:T(8,128)(2,1)S(1)} %all_gather.19), channel_id=1, source_target_pairs={{0,8},{8,0},{16,24},{24,16},{32,40},{40,32},{48,56},{56,48},{64,72... | collective-permute-start | bytes 196616 | tf_op jit(solution)/shard_map/ppermute | solution.py:16
  65.9 6.2 %collective-permute-start.2 = (bf16[256,128]{1,0:T(8,128)(2,1)S(1)}, bf16[256,128]{1,0:T(8,128)(2,1)S(1)}, u32[]{:S(2)}, u32[]{:S(2)}) collective-permute-start(bf16[256,128]{1,0:T(8,128)(2,1)S(1)} %all_gather.20), channel_id=1, source_target_pairs={{0,8},{8,0},{16,24},{24,16},{32,40},{40,32},{48,56},{56,48},{64,72... | collective-permute-start | bytes 196616 | tf_op jit(solution)/shard_map/ppermute | solution.py:16
  72.2 8.4 %collective-permute-start.3 = (bf16[512,128]{1,0:T(8,128)(2,1)S(1)}, bf16[512,128]{1,0:T(8,128)(2,1)S(1)}, u32[]{:S(2)}, u32[]{:S(2)}) collective-permute-start(bf16[512,128]{1,0:T(8,128)(2,1)S(1)} %maximum_select_fusion.15), channel_id=1, source_target_pairs={{0,16},{16,0},{8,24},{24,8},{32,48},{48,32},{40,56},{56,40},{64,80... | collective-permute-start | bytes 393224 | tf_op jit(solution)/shard_map/ppermute | solution.py:16
  93.5 6.2 %collective-permute-start.4 = (bf16[256,128]{1,0:T(8,128)(2,1)S(1)}, bf16[256,128]{1,0:T(8,128)(2,1)S(1)}, u32[]{:S(2)}, u32[]{:S(2)}) collective-permute-start(bf16[256,128]{1,0:T(8,128)(2,1)S(1)} %all_gather.21), channel_id=1, source_target_pairs={{0,8},{8,0},{16,24},{24,16},{32,40},{40,32},{48,56},{56,48},{64,72... | collective-permute-start | bytes 196616 | tf_op jit(solution)/shard_map/ppermute | solution.py:16
  99.7 8.4 %collective-permute-start.5 = (bf16[512,128]{1,0:T(8,128)(2,1)S(1)}, bf16[512,128]{1,0:T(8,128)(2,1)S(1)}, u32[]{:S(2)}, u32[]{:S(2)}) collective-permute-start(bf16[512,128]{1,0:T(8,128)(2,1)S(1)} %maximum_select_fusion.16), channel_id=1, source_target_pairs={{0,16},{16,0},{8,24},{24,8},{32,48},{48,32},{40,56},{56,40},{64,80... | collective-permute-start | bytes 393224 | tf_op jit(solution)/shard_map/ppermute | solution.py:16
  109.1 72.2 %copy-start.5 = (bf16[3,32,128]{2,1,0:T(8,128)(2,1)S(1)}, bf16[3,32,128]{2,1,0:T(8,128)(2,1)}, u32[]{:S(2)}) copy-start(bf16[3,32,128]{2,1,0:T(8,128)(2,1)} %param.18) | copy-start | bytes 73732
  121.9 6.2 %collective-permute-start.6 = (bf16[256,128]{1,0:T(8,128)(2,1)S(1)}, bf16[256,128]{1,0:T(8,128)(2,1)S(1)}, u32[]{:S(2)}, u32[]{:S(2)}) collective-permute-start(bf16[256,128]{1,0:T(8,128)(2,1)S(1)} %all_gather.22), channel_id=1, source_target_pairs={{0,8},{8,0},{16,24},{24,16},{32,40},{40,32},{48,56},{56,48},{64,72... | collective-permute-start | bytes 196616 | tf_op jit(solution)/shard_map/ppermute | solution.py:16
  128.1 8.4 %collective-permute-start.7 = (bf16[512,128]{1,0:T(8,128)(2,1)S(1)}, bf16[512,128]{1,0:T(8,128)(2,1)S(1)}, u32[]{:S(2)}, u32[]{:S(2)}) collective-permute-start(bf16[512,128]{1,0:T(8,128)(2,1)S(1)} %maximum_select_fusion.17), channel_id=1, source_target_pairs={{0,16},{16,0},{8,24},{24,8},{32,48},{48,32},{40,56},{56,40},{64,80... | collective-permute-start | bytes 393224 | tf_op jit(solution)/shard_map/ppermute | solution.py:16
  136.6 8.5 %collective-permute-start.8 = (bf16[1024,128]{1,0:T(8,128)(2,1)S(1)}, bf16[1024,128]{1,0:T(8,128)(2,1)S(1)}, u32[]{:S(2)}, u32[]{:S(2)}) collective-permute-start(bf16[1024,128]{1,0:T(8,128)(2,1)S(1)} %maximum_select_fusion.9), channel_id=1, source_target_pairs={{0,32},{32,0},{8,40},{40,8},{16,48},{48,16},{24,56},{56,24},{64,96... | collective-permute-start | bytes 786440 | tf_op jit(solution)/shard_map/ppermute | solution.py:16
  158.0 6.2 %collective-permute-start.9 = (bf16[256,128]{1,0:T(8,128)(2,1)S(1)}, bf16[256,128]{1,0:T(8,128)(2,1)S(1)}, u32[]{:S(2)}, u32[]{:S(2)}) collective-permute-start(bf16[256,128]{1,0:T(8,128)(2,1)S(1)} %all_gather.23), channel_id=1, source_target_pairs={{0,8},{8,0},{16,24},{24,16},{32,40},{40,32},{48,56},{56,48},{64,72... | collective-permute-start | bytes 196616 | tf_op jit(solution)/shard_map/ppermute | solution.py:16
  164.3 8.4 %collective-permute-start.10 = (bf16[512,128]{1,0:T(8,128)(2,1)S(1)}, bf16[512,128]{1,0:T(8,128)(2,1)S(1)}, u32[]{:S(2)}, u32[]{:S(2)}) collective-permute-start(bf16[512,128]{1,0:T(8,128)(2,1)S(1)} %maximum_select_fusion.18), channel_id=1, source_target_pairs={{0,16},{16,0},{8,24},{24,8},{32,48},{48,32},{40,56},{56,40},{64,80... | collective-permute-start | bytes 393224 | tf_op jit(solution)/shard_map/ppermute | solution.py:16
  172.7 2.2 copy-start.1
  172.7 8.6 %collective-permute-start.11 = (bf16[1024,128]{1,0:T(8,128)(2,1)S(1)}, bf16[1024,128]{1,0:T(8,128)(2,1)}, u32[]{:S(2)}, u32[]{:S(2)}) collective-permute-start(bf16[1024,128]{1,0:T(8,128)(2,1)S(1)} %maximum_select_fusion.10), channel_id=1, source_target_pairs={{0,32},{32,0},{8,40},{40,8},{16,48},{48,16},{24,56},{56,24},{64,96... | collective-permute-start | bytes 786440 | tf_op jit(solution)/shard_map/ppermute | solution.py:16
  183.3 13.2 %collective-permute-start.12 = (f32[1024,128]{0,1:T(8,128)S(1)}, f32[1024,128]{0,1:T(8,128)S(1)}, u32[]{:S(2)}, u32[]{:S(2)}) collective-permute-start(f32[1024,128]{0,1:T(8,128)S(1)} %slice_select_fusion.1), channel_id=1, source_target_pairs={{0,32},{32,0},{8,40},{40,8},{16,48},{48,16},{24,56},{56,24},{64,96... | collective-permute-start | bytes 1572872 | tf_op jit(solution)/shard_map/ppermute | solution.py:16
  196.5 56.8 %copy-start.4 = (bf16[32,3584]{1,0:T(8,128)(2,1)S(1)}, bf16[32,3584]{1,0:T(8,128)(2,1)}, u32[]{:S(2)}) copy-start(bf16[32,3584]{1,0:T(8,128)(2,1)} %param.16) | copy-start | bytes 688132
  196.6 10.5 %collective-permute-start.13 = (f32[512,128]{0,1:T(8,128)S(1)}, f32[512,128]{0,1:T(8,128)S(1)}, u32[]{:S(2)}, u32[]{:S(2)}) collective-permute-start(f32[512,128]{0,1:T(8,128)S(1)} %slice_select_fusion.5), channel_id=1, source_target_pairs={{0,16},{16,0},{8,24},{24,8},{32,48},{48,32},{40,56},{56,40},{64,80... | collective-permute-start | bytes 786440 | tf_op jit(solution)/shard_map/ppermute | solution.py:16
  207.2 6.9 %collective-permute-start.14 = (f32[256,128]{0,1:T(8,128)S(1)}, f32[256,128]{0,1:T(8,128)S(1)}, u32[]{:S(2)}, u32[]{:S(2)}) collective-permute-start(f32[256,128]{0,1:T(8,128)S(1)} %slice_select_fusion.11), channel_id=1, source_target_pairs={{0,8},{8,0},{16,24},{24,16},{32,40},{40,32},{48,56},{56,48},{64,72... | collective-permute-start | bytes 393224 | tf_op jit(solution)/shard_map/ppermute | solution.py:16
  214.8 111.4 %reduce-scatter.21.cloned.1.call-start = ((), (), s32[]{:S(2)}) async-start(), calls=%async_computation.7 | async-start | bytes 147456 | tf_op jit(solution)/shard_map/reduce_scatter | solution.py:50
  253.7 13.1 %collective-permute-start.15 = (f32[1024,128]{0,1:T(8,128)S(1)}, f32[1024,128]{0,1:T(8,128)S(1)}, u32[]{:S(2)}, u32[]{:S(2)}) collective-permute-start(f32[1024,128]{0,1:T(8,128)S(1)} %slice_select_fusion), channel_id=1, source_target_pairs={{0,32},{32,0},{8,40},{40,8},{16,48},{48,16},{24,56},{56,24},{64,96... | collective-permute-start | bytes 1572872 | tf_op jit(solution)/shard_map/ppermute | solution.py:16
  266.9 9.8 %collective-permute-start.16 = (f32[512,128]{0,1:T(8,128)S(1)}, f32[512,128]{0,1:T(8,128)S(1)}, u32[]{:S(2)}, u32[]{:S(2)}) collective-permute-start(f32[512,128]{0,1:T(8,128)S(1)} %slice_select_fusion.4), channel_id=1, source_target_pairs={{0,16},{16,0},{8,24},{24,8},{32,48},{48,32},{40,56},{56,40},{64,80... | collective-permute-start | bytes 786440 | tf_op jit(solution)/shard_map/ppermute | solution.py:16
  276.7 6.9 %collective-permute-start.17 = (f32[256,128]{0,1:T(8,128)S(1)}, f32[256,128]{0,1:T(8,128)S(1)}, u32[]{:S(2)}, u32[]{:S(2)}) collective-permute-start(f32[256,128]{0,1:T(8,128)S(1)} %slice_select_fusion.10), channel_id=1, source_target_pairs={{0,8},{8,0},{16,24},{24,16},{32,40},{40,32},{48,56},{56,48},{64,72... | collective-permute-start | bytes 393224 | tf_op jit(solution)/shard_map/ppermute | solution.py:16
  284.4 99.9 %reduce-scatter.23.cloned.1.call-start = ((), (), s32[]{:S(2)}) async-start(), calls=%async_computation.8 | async-start | bytes 147456
  327.4 9.8 %collective-permute-start.18 = (f32[512,128]{0,1:T(8,128)S(1)}, f32[512,128]{0,1:T(8,128)S(1)}, u32[]{:S(2)}, u32[]{:S(2)}) collective-permute-start(f32[512,128]{0,1:T(8,128)S(1)} %slice_select_fusion.3), channel_id=1, source_target_pairs={{0,16},{16,0},{8,24},{24,8},{32,48},{48,32},{40,56},{56,40},{64,80... | collective-permute-start | bytes 786440 | tf_op jit(solution)/shard_map/ppermute | solution.py:16
  337.2 6.9 %collective-permute-start.19 = (f32[256,128]{0,1:T(8,128)S(1)}, f32[256,128]{0,1:T(8,128)S(1)}, u32[]{:S(2)}, u32[]{:S(2)}) collective-permute-start(f32[256,128]{0,1:T(8,128)S(1)} %slice_select_fusion.9), channel_id=1, source_target_pairs={{0,8},{8,0},{16,24},{24,16},{32,40},{40,32},{48,56},{56,48},{64,72... | collective-permute-start | bytes 393224 | tf_op jit(solution)/shard_map/ppermute | solution.py:16
  344.9 97.6 %reduce-scatter.25.cloned.1.call-start = ((), (), s32[]{:S(2)}) async-start(), calls=%async_computation.9 | async-start | bytes 147456 | tf_op jit(solution)/shard_map/reduce_scatter | solution.py:50
  385.3 65.9 %copy-start.6 = (bf16[3,32]{1,0:T(4,128)(2,1)S(1)}, bf16[3,32]{1,0:T(4,128)(2,1)}, u32[]{:S(2)}) copy-start(bf16[3,32]{1,0:T(4,128)(2,1)} %param.19) | copy-start | bytes 580
  385.3 65.9 %copy-start.2 = (bf16[1024,128]{1,0:T(8,128)(2,1)S(1)}, bf16[1024,128]{1,0:T(8,128)(2,1)}, u32[]{:S(2)}) copy-start(bf16[1024,128]{1,0:T(8,128)(2,1)} %param.13) | copy-start | bytes 786436
  385.4 66.1 %copy-start.7 = (bf16[1024]{0:T(1024)(128)(2,1)S(1)}, bf16[1024]{0:T(1024)(128)(2,1)}, u32[]{:S(2)}) copy-start(bf16[1024]{0:T(1024)(128)(2,1)} %param.14) | copy-start | bytes 6148
  385.4 9.9 %collective-permute-start.20 = (f32[512,128]{0,1:T(8,128)S(1)}, f32[512,128]{0,1:T(8,128)S(1)}, u32[]{:S(2)}, u32[]{:S(2)}) collective-permute-start(f32[512,128]{0,1:T(8,128)S(1)} %slice_select_fusion.2), channel_id=1, source_target_pairs={{0,16},{16,0},{8,24},{24,8},{32,48},{48,32},{40,56},{56,40},{64,80... | collective-permute-start | bytes 786440 | tf_op jit(solution)/shard_map/ppermute | solution.py:16
  395.4 6.9 %collective-permute-start.21 = (f32[256,128]{0,1:T(8,128)S(1)}, f32[256,128]{0,1:T(8,128)S(1)}, u32[]{:S(2)}, u32[]{:S(2)}) collective-permute-start(f32[256,128]{0,1:T(8,128)S(1)} %slice_select_fusion.8), channel_id=1, source_target_pairs={{0,8},{8,0},{16,24},{24,16},{32,40},{40,32},{48,56},{56,48},{64,72... | collective-permute-start | bytes 393224 | tf_op jit(solution)/shard_map/ppermute | solution.py:16
  403.0 85.7 %reduce-scatter.27.cloned.1.call-start = ((), (), s32[]{:S(2)}) async-start(), calls=%async_computation.10 | async-start | bytes 147456
  443.5 6.9 %collective-permute-start.22 = (f32[256,128]{0,1:T(8,128)S(1)}, f32[256,128]{0,1:T(8,128)S(1)}, u32[]{:S(2)}, u32[]{:S(2)}) collective-permute-start(f32[256,128]{0,1:T(8,128)S(1)} %slice_select_fusion.7), channel_id=1, source_target_pairs={{0,8},{8,0},{16,24},{24,16},{32,40},{40,32},{48,56},{56,48},{64,72... | collective-permute-start | bytes 393224 | tf_op jit(solution)/shard_map/ppermute | solution.py:16
  451.2 83.6 %reduce-scatter.29.cloned.1.call-start = ((), (), s32[]{:S(2)}) async-start(), calls=%async_computation.11 | async-start | bytes 147456
  489.7 6.9 %collective-permute-start.23 = (f32[256,128]{0,1:T(8,128)S(1)}, f32[256,128]{0,1:T(8,128)S(1)}, u32[]{:S(2)}, u32[]{:S(2)}) collective-permute-start(f32[256,128]{0,1:T(8,128)S(1)} %slice_select_fusion.6), channel_id=1, source_target_pairs={{0,8},{8,0},{16,24},{24,16},{32,40},{40,32},{48,56},{56,48},{64,72... | collective-permute-start | bytes 393224 | tf_op jit(solution)/shard_map/ppermute | solution.py:16
Sparse Core Ops, SparseCore 0:
  215.0 37.4 reduce-scatter.18
  284.5 41.6 reduce-scatter.20
  345.0 39.2 reduce-scatter.22
  403.1 39.3 reduce-scatter.24
  451.3 37.3 reduce-scatter.26
  497.5 37.2 reduce-scatter.28
where the time goes:
time: 545 us; the launch traced here: 544 us
  waiting for transfers between devices  355 us (65%)
  blocking collectives  76.8 us (14%)
  starting transfers between devices  76.1 us (14%)
  between operations  15.5 us (3%)
  local copies, waits for them, and re-layouts  10.3 us (2%)
  matrix products  8.35 us (2%)
    unnamed x10, waiting for transfers between devices  151 us
    ppermute x24, waiting for transfers between devices, from_partner(): return lax.ppermute(block, axis, route)  123 us
    reduce_scatter x2, waiting for transfers between devices, group_reduce(): return lax.psum_scatter(reduced, 'sec', scatter_dimension=0, tiled=True)  81.2 us
    all_gather x6, blocking collectives, group_gather(): block = lax.all_gather(piece, 'sec', axis=0, tiled=True)  76.8 us
    ppermute x24, starting transfers between devices, from_partner(): return lax.ppermute(block, axis, route)  75.9 us
  transfers between devices with their start and end apart: 30, of which 30 were waited for; matrix products, arithmetic and copies ran while one was open for 0% of the time, Pallas kernels for 0%

commit v1 on v0

--- a/solution.py
+++ b/solution.py
@@ -4,6 +4,24 @@
 from jax.sharding import PartitionSpec as P
 
 BLOCK = 128
+
+
+def gather_around(array, axis, dim):
+    ways, here, step = (lax.axis_size(axis), lax.axis_index(axis), array.shape[dim])
+    dims = [n * ways if d == dim else n for d, n in enumerate(array.shape)]
+    full = lax.dynamic_update_slice_in_dim(
+        jnp.zeros(dims, array.dtype), array, here * step, axis=dim
+    )
+    going_up = going_down = array
+    for far in range(1, ways // 2 + 1):
+        going_up = lax.ppermute(going_up, axis, [(d, (d + 1) % ways) for d in range(ways)])
+        full = lax.dynamic_update_slice_in_dim(full, going_up, (here - far) % ways * step, axis=dim)
+        if 2 * far < ways:
+            going_down = lax.ppermute(going_down, axis, [(d, (d - 1) % ways) for d in range(ways)])
+            full = lax.dynamic_update_slice_in_dim(
+                full, going_down, (here + far) % ways * step, axis=dim
+            )
+    return full
 
 
 def from_partner(block, axis, apart):
@@ -28,7 +46,7 @@
 
 
 def group_gather(piece, height):
-    block = lax.all_gather(piece, "sec", axis=0, tiled=True)
+    block = gather_around(piece, "sec", 0)
     return pair_gather(block, height)
 
 

time: 545 us -> 578 us (1.061)
  blocking collectives: 76.8 us -> 0 us
  starting transfers between devices: 76.1 us -> 132 us
  waiting for transfers between devices: 355 us -> 386 us
  local copies, waits for them, and re-layouts: 10.3 us -> 32.6 us
    all_gather x6 -> x0, blocking collectives: 76.8 us -> none  [group_gather(): block = lax.all_gather(piece, 'sec', axis=0, tiled=True)]
    ppermute x0 -> x42, starting transfers between devices: none -> 53 us  [the longest x18 52.8 us: gather_around(): lax.ppermute(going_down, axis, [(d, (d - 1) % ways) for d in range(ways)])]
    ppermute x0 -> x42, waiting for transfers between devices: none -> 29.9 us  [the longest x24 29.6 us: gather_around(): lax.ppermute(going_up, axis, [(d, (d + 1) % ways) for d in range(ways)])]
    dynamic_update_slice x0 -> x48, local copies, waits for them, and re-layouts: none -> 17.5 us  [the longest x24 8.39 us: gather_around(): lax.dynamic_update_slice_in_dim(full, going_up, (here - far) % ways * ste...]
  transfers between devices with their start and end apart: 30 -> 72, of which waited for: 30 -> 54; matrix products, arithmetic and copies ran while one was open for 0% -> 4% of each run, Pallas kernels for 0% -> 0%
where the time goes in v1:
time: 578 us; the launch traced here: 577 us
  waiting for transfers between devices  386 us (67%)
  starting transfers between devices  132 us (23%)
  local copies, waits for them, and re-layouts  32.6 us (6%)
  between operations  16.1 us (3%)
  matrix products  8.47 us (1%)
    unnamed x10, waiting for transfers between devices  155 us
    ppermute x24, waiting for transfers between devices, from_partner(): return lax.ppermute(block, axis, route)  120 us
    reduce_scatter x2, waiting for transfers between devices, group_reduce(): return lax.psum_scatter(reduced, 'sec', scatter_dimension=0, tiled=True)  81.1 us
    ppermute x24, starting transfers between devices, from_partner(): return lax.ppermute(block, axis, route)  78.5 us
    ppermute x18, starting transfers between devices, gather_around(): lax.ppermute(going_down, axis, [(d, (d - 1) % ways) for d in range(ways)])  52.8 us
    ppermute x24, waiting for transfers between devices, gather_around(): lax.ppermute(going_up, axis, [(d, (d + 1) % ways) for d in range(ways)])  29.6 us
  transfers between devices with their start and end apart: 72, of which 54 were waited for; matrix products, arithmetic and copies ran while one was open for 4% of the time, Pallas kernels for 0%

profile of v1, /device:TPU:8, one launch (start us, length us, event | category | flops | bytes accessed | tf_op | source)
XLA Modules:
  0.0 576.9 jit_solution(15865627466089217905)
XLA Ops:
  10.1 2.9 collective-permute-start.1
  14.6 3.0 collective-permute-start.3
  19.2 3.0 collective-permute-start.5
  28.5 7.7 %collective-permute-start.7 = (bf16[256,128]{0,1:T(8,128)(2,1)S(1)}, bf16[256,128]{0,1:T(8,128)(2,1)S(1)}, u32[]{:S(2)}, u32[]{:S(2)}) collective-permute-start(bf16[256,128]{0,1:T(8,128)(2,1)S(1)} %dynamic_update_slice.151), channel_id=1, source_target_pairs={{0,8},{8,0},{16,24},{24,16},{32,40},{40,32},{48,56},{56,48},{64,72... | collective-permute-start | bytes 196616 | tf_op jit(solution)/shard_map/ppermute | solution.py:34
  38.6 2.9 collective-permute-start.9
  42.9 2.9 collective-permute-start.11
  56.1 3.9 collective-permute-start.15
  63.2 2.9 collective-permute-start.17
  67.5 2.9 collective-permute-start.19
  80.6 3.9 collective-permute-start.23
  89.2 6.3 %collective-permute-done.24 = bf16[512,128]{0,1:T(8,128)(2,1)S(1)} collective-permute-done((bf16[512,128]{0,1:T(8,128)(2,1)S(1)}, bf16[512,128]{0,1:T(8,128)(2,1)S(1)}, u32[]{:S(2)}, u32[]{:S(2)}) %collective-permute-start.24) | collective-permute-done | bytes 131104 | tf_op jit(solution)/shard_map/ppermute | solution.py:34
  95.6 3.0 collective-permute-start.26
  99.9 2.9 collective-permute-start.28
  113.1 4.4 collective-permute-start.32
  121.9 6.4 %collective-permute-done.33 = bf16[512,128]{0,1:T(8,128)(2,1)S(1)} collective-permute-done((bf16[512,128]{0,1:T(8,128)(2,1)S(1)}, bf16[512,128]{0,1:T(8,128)(2,1)S(1)}, u32[]{:S(2)}, u32[]{:S(2)}) %collective-permute-start.33) | collective-permute-done | bytes 131104 | tf_op jit(solution)/shard_map/ppermute | solution.py:34
  129.4 3.0 collective-permute-start.35
  133.7 2.9 collective-permute-start.37
  146.9 4.4 collective-permute-start.41
  155.7 6.4 %collective-permute-done.42 = bf16[512,128]{0,1:T(8,128)(2,1)S(1)} collective-permute-done((bf16[512,128]{0,1:T(8,128)(2,1)S(1)}, bf16[512,128]{0,1:T(8,128)(2,1)S(1)}, u32[]{:S(2)}, u32[]{:S(2)}) %collective-permute-start.42) | collective-permute-done | bytes 131104 | tf_op jit(solution)/shard_map/ppermute | solution.py:34
  164.2 6.3 %collective-permute-done.43 = bf16[1024,128]{0,1:T(8,128)(2,1)S(1)} collective-permute-done((bf16[1024,128]{0,1:T(8,128)(2,1)S(1)}, bf16[1024,128]{0,1:T(8,128)(2,1)S(1)}, u32[]{:S(2)}, u32[]{:S(2)}) %collective-permute-start.43) | collective-permute-done | bytes 262176 | tf_op jit(solution)/shard_map/ppermute | solution.py:34
  170.8 3.0 collective-permute-start.45
  188.3 4.4 collective-permute-start.51
  197.1 6.4 %collective-permute-done.52 = bf16[512,128]{0,1:T(8,128)(2,1)S(1)} collective-permute-done((bf16[512,128]{0,1:T(8,128)(2,1)S(1)}, bf16[512,128]{0,1:T(8,128)(2,1)S(1)}, u32[]{:S(2)}, u32[]{:S(2)}) %collective-permute-start.52) | collective-permute-done | bytes 131104 | tf_op jit(solution)/shard_map/ppermute | solution.py:34
  205.6 6.4 %collective-permute-done.53 = bf16[1024,128]{0,1:T(8,128)(2,1)} collective-permute-done((bf16[1024,128]{0,1:T(8,128)(2,1)S(1)}, bf16[1024,128]{0,1:T(8,128)(2,1)}, u32[]{:S(2)}, u32[]{:S(2)}) %collective-permute-start.53) | collective-permute-done | bytes 262176 | tf_op jit(solution)/shard_map/ppermute | solution.py:34
  216.0 9.1 %collective-permute-done.54 = f32[1024,128]{0,1:T(8,128)S(1)} collective-permute-done((f32[1024,128]{0,1:T(8,128)S(1)}, f32[1024,128]{0,1:T(8,128)S(1)}, u32[]{:S(2)}, u32[]{:S(2)}) %collective-permute-start.54) | collective-permute-done | bytes 524320 | tf_op jit(solution)/shard_map/ppermute | solution.py:34
  227.3 7.8 %collective-permute-done.55 = f32[512,128]{0,1:T(8,128)S(1)} collective-permute-done((f32[512,128]{0,1:T(8,128)S(1)}, f32[512,128]{0,1:T(8,128)S(1)}, u32[]{:S(2)}, u32[]{:S(2)}) %collective-permute-start.55) | collective-permute-done | bytes 262176 | tf_op jit(solution)/shard_map/ppermute | solution.py:34
  235.2 4.7 collective-permute-start.56
  240.0 2.9 collective-permute-done.56
  243.8 41.8 %reduce-scatter.19.cloned.1.call-done = f32[32,128]{1,0:T(8,128)} async-done(((f32[256,128]{1,0:T(8,128)}), f32[32,128]{1,0:T(8,128)}) %reduce-scatter.19.cloned.1.call-update) | async-done | bytes 16400
  286.8 3.7 collective-permute-start.57
  290.5 9.3 %collective-permute-done.57 = f32[1024,128]{0,1:T(8,128)S(1)} collective-permute-done((f32[1024,128]{0,1:T(8,128)S(1)}, f32[1024,128]{0,1:T(8,128)S(1)}, u32[]{:S(2)}, u32[]{:S(2)}) %collective-permute-start.57) | collective-permute-done | bytes 524320 | tf_op jit(solution)/shard_map/ppermute | solution.py:34
  299.9 4.0 collective-permute-start.58
  304.0 5.7 collective-permute-done.58
  309.8 3.5 collective-permute-start.59
  313.3 3.4 collective-permute-done.59
  317.5 41.7 %reduce-scatter.21.cloned.1.call-done = f32[32,128]{1,0:T(8,128)} async-done(((f32[256,128]{1,0:T(8,128)}), f32[32,128]{1,0:T(8,128)}) %reduce-scatter.21.cloned.1.call-update) | async-done | bytes 16400 | tf_op jit(solution)/shard_map/reduce_scatter | solution.py:68
  360.4 4.0 collective-permute-start.60
  364.4 5.8 collective-permute-done.60
  372.8 4.3 collective-permute-done.61
  378.0 39.4 %reduce-scatter.23.cloned.1.call-done = f32[32,128]{1,0:T(8,128)} async-done(((f32[256,128]{1,0:T(8,128)}), f32[32,128]{1,0:T(8,128)}) %reduce-scatter.23.cloned.1.call-update) | async-done | bytes 16400
  418.5 4.1 collective-permute-start.62
  422.6 5.8 %collective-permute-done.62 = f32[512,128]{0,1:T(8,128)S(1)} collective-permute-done((f32[512,128]{0,1:T(8,128)S(1)}, f32[512,128]{0,1:T(8,128)S(1)}, u32[]{:S(2)}, u32[]{:S(2)}) %collective-permute-start.62) | collective-permute-done | bytes 262176 | tf_op jit(solution)/shard_map/ppermute | solution.py:34
  431.1 4.3 collective-permute-done.63
  436.2 39.4 %reduce-scatter.25.cloned.1.call-done = f32[32,128]{1,0:T(8,128)} async-done(((f32[256,128]{1,0:T(8,128)}), f32[32,128]{1,0:T(8,128)}) %reduce-scatter.25.cloned.1.call-update) | async-done | bytes 16400 | tf_op jit(solution)/shard_map/reduce_scatter | solution.py:68
  479.1 4.4 collective-permute-done.64
  484.6 37.0 %reduce-scatter.27.cloned.1.call-done = f32[32,128]{1,0:T(8,128)} async-done(((f32[256,128]{1,0:T(8,128)}), f32[32,128]{1,0:T(8,128)}) %reduce-scatter.27.cloned.1.call-update) | async-done | bytes 16400
  525.2 4.3 collective-permute-done.65
  531.0 36.9 %reduce-scatter.29.cloned.1.call-done = f32[32,128]{1,0:T(8,128)} async-done(((f32[256,128]{1,0:T(8,128)}), f32[32,128]{1,0:T(8,128)}) %reduce-scatter.29.cloned.1.call-update) | async-done | bytes 16400
  (281 shorter events, 131.0 us)
Async XLA Ops:
  7.2 278.4 %reduce-scatter.19.cloned.1.call-start = ((), (), s32[]{:S(2)}) async-start(), calls=%async_computation.6 | async-start | bytes 147456
  10.1 4.6 collective-permute-start
  10.1 4.5 collective-permute-start.1
  14.6 4.6 collective-permute-start.2
  14.6 4.6 collective-permute-start.3
  19.2 4.6 collective-permute-start.4
  19.2 7.0 %collective-permute-start.5 = (bf16[32,128]{0,1:T(8,128)(2,1)S(1)}, bf16[32,128]{0,1:T(8,128)(2,1)S(1)}, u32[]{:S(2)}, u32[]{:S(2)}) collective-permute-start(bf16[32,128]{0,1:T(8,128)(2,1)S(1)} %collective-permute-done.3), channel_id=1, source_target_pairs={{0,7},{1,0},{2,1},{3,2},{4,3},{5,4},{6,5},{7,6},{8,15},{9,8},{10,9... | collective-permute-start | bytes 24584 | tf_op jit(solution)/shard_map/ppermute | solution.py:20
  23.7 4.6 collective-permute-start.6
  28.5 10.0 %collective-permute-start.7 = (bf16[256,128]{0,1:T(8,128)(2,1)S(1)}, bf16[256,128]{0,1:T(8,128)(2,1)S(1)}, u32[]{:S(2)}, u32[]{:S(2)}) collective-permute-start(bf16[256,128]{0,1:T(8,128)(2,1)S(1)} %dynamic_update_slice.151), channel_id=1, source_target_pairs={{0,8},{8,0},{16,24},{24,16},{32,40},{40,32},{48,56},{56,48},{64,72... | collective-permute-start | bytes 196616 | tf_op jit(solution)/shard_map/ppermute | solution.py:34
  38.6 4.3 collective-permute-start.9
  47.2 7.3 %collective-permute-start.13 = (bf16[32,128]{1,0:T(8,128)(2,1)S(1)}, bf16[32,128]{1,0:T(8,128)(2,1)S(1)}, u32[]{:S(2)}, u32[]{:S(2)}) collective-permute-start(bf16[32,128]{1,0:T(8,128)(2,1)S(1)} %collective-permute-done.11), channel_id=1, source_target_pairs={{0,7},{1,0},{2,1},{3,2},{4,3},{5,4},{6,5},{7,6},{8,15},{9,8},{10,9... | collective-permute-start | bytes 24584 | tf_op jit(solution)/shard_map/ppermute | solution.py:20
  56.1 6.2 %collective-permute-start.15 = (bf16[256,128]{0,1:T(8,128)(2,1)S(1)}, bf16[256,128]{0,1:T(8,128)(2,1)S(1)}, u32[]{:S(2)}, u32[]{:S(2)}) collective-permute-start(bf16[256,128]{0,1:T(8,128)(2,1)S(1)} %dynamic_update_slice.159), channel_id=1, source_target_pairs={{0,8},{8,0},{16,24},{24,16},{32,40},{40,32},{48,56},{56,48},{64,72... | collective-permute-start | bytes 196616 | tf_op jit(solution)/shard_map/ppermute | solution.py:34
  63.2 4.3 collective-permute-start.17
  71.8 7.3 %collective-permute-start.21 = (bf16[32,128]{1,0:T(8,128)(2,1)S(1)}, bf16[32,128]{1,0:T(8,128)(2,1)S(1)}, u32[]{:S(2)}, u32[]{:S(2)}) collective-permute-start(bf16[32,128]{1,0:T(8,128)(2,1)S(1)} %collective-permute-done.19), channel_id=1, source_target_pairs={{0,7},{1,0},{2,1},{3,2},{4,3},{5,4},{6,5},{7,6},{8,15},{9,8},{10,9... | collective-permute-start | bytes 24584 | tf_op jit(solution)/shard_map/ppermute | solution.py:20
  80.6 6.4 %collective-permute-start.23 = (bf16[256,128]{0,1:T(8,128)(2,1)S(1)}, bf16[256,128]{0,1:T(8,128)(2,1)S(1)}, u32[]{:S(2)}, u32[]{:S(2)}) collective-permute-start(bf16[256,128]{0,1:T(8,128)(2,1)S(1)} %dynamic_update_slice.167), channel_id=1, source_target_pairs={{0,8},{8,0},{16,24},{24,16},{32,40},{40,32},{48,56},{56,48},{64,72... | collective-permute-start | bytes 196616 | tf_op jit(solution)/shard_map/ppermute | solution.py:34
  87.0 8.4 %collective-permute-start.24 = (bf16[512,128]{0,1:T(8,128)(2,1)S(1)}, bf16[512,128]{0,1:T(8,128)(2,1)S(1)}, u32[]{:S(2)}, u32[]{:S(2)}) collective-permute-start(bf16[512,128]{0,1:T(8,128)(2,1)S(1)} %maximum_select_fusion.15), channel_id=1, source_target_pairs={{0,16},{16,0},{8,24},{24,8},{32,48},{48,32},{40,56},{56,40},{64,80... | collective-permute-start | bytes 393224 | tf_op jit(solution)/shard_map/ppermute | solution.py:34
  95.6 4.3 collective-permute-start.26
  104.2 7.3 %collective-permute-start.30 = (bf16[32,128]{1,0:T(8,128)(2,1)S(1)}, bf16[32,128]{1,0:T(8,128)(2,1)S(1)}, u32[]{:S(2)}, u32[]{:S(2)}) collective-permute-start(bf16[32,128]{1,0:T(8,128)(2,1)S(1)} %collective-permute-done.28), channel_id=1, source_target_pairs={{0,7},{1,0},{2,1},{3,2},{4,3},{5,4},{6,5},{7,6},{8,15},{9,8},{10,9... | collective-permute-start | bytes 24584 | tf_op jit(solution)/shard_map/ppermute | solution.py:20
  113.1 6.9 %collective-permute-start.32 = (bf16[256,128]{0,1:T(8,128)(2,1)S(1)}, bf16[256,128]{0,1:T(8,128)(2,1)S(1)}, u32[]{:S(2)}, u32[]{:S(2)}) collective-permute-start(bf16[256,128]{0,1:T(8,128)(2,1)S(1)} %dynamic_update_slice.175), channel_id=1, source_target_pairs={{0,8},{8,0},{16,24},{24,16},{32,40},{40,32},{48,56},{56,48},{64,72... | collective-permute-start | bytes 196616 | tf_op jit(solution)/shard_map/ppermute | solution.py:34
  120.0 8.4 %collective-permute-start.33 = (bf16[512,128]{0,1:T(8,128)(2,1)S(1)}, bf16[512,128]{0,1:T(8,128)(2,1)S(1)}, u32[]{:S(2)}, u32[]{:S(2)}) collective-permute-start(bf16[512,128]{0,1:T(8,128)(2,1)S(1)} %maximum_select_fusion.16), channel_id=1, source_target_pairs={{0,16},{16,0},{8,24},{24,8},{32,48},{48,32},{40,56},{56,40},{64,80... | collective-permute-start | bytes 393224 | tf_op jit(solution)/shard_map/ppermute | solution.py:34
  129.4 4.3 collective-permute-start.35
  138.0 7.3 %collective-permute-start.39 = (bf16[32,128]{1,0:T(8,128)(2,1)S(1)}, bf16[32,128]{1,0:T(8,128)(2,1)S(1)}, u32[]{:S(2)}, u32[]{:S(2)}) collective-permute-start(bf16[32,128]{1,0:T(8,128)(2,1)S(1)} %collective-permute-done.37), channel_id=1, source_target_pairs={{0,7},{1,0},{2,1},{3,2},{4,3},{5,4},{6,5},{7,6},{8,15},{9,8},{10,9... | collective-permute-start | bytes 24584 | tf_op jit(solution)/shard_map/ppermute | solution.py:20
  146.9 6.9 %collective-permute-start.41 = (bf16[256,128]{0,1:T(8,128)(2,1)S(1)}, bf16[256,128]{0,1:T(8,128)(2,1)S(1)}, u32[]{:S(2)}, u32[]{:S(2)}) collective-permute-start(bf16[256,128]{0,1:T(8,128)(2,1)S(1)} %dynamic_update_slice.183), channel_id=1, source_target_pairs={{0,8},{8,0},{16,24},{24,16},{32,40},{40,32},{48,56},{56,48},{64,72... | collective-permute-start | bytes 196616 | tf_op jit(solution)/shard_map/ppermute | solution.py:34
  153.8 8.4 %collective-permute-start.42 = (bf16[512,128]{0,1:T(8,128)(2,1)S(1)}, bf16[512,128]{0,1:T(8,128)(2,1)S(1)}, u32[]{:S(2)}, u32[]{:S(2)}) collective-permute-start(bf16[512,128]{0,1:T(8,128)(2,1)S(1)} %maximum_select_fusion.17), channel_id=1, source_target_pairs={{0,16},{16,0},{8,24},{24,8},{32,48},{48,32},{40,56},{56,40},{64,80... | collective-permute-start | bytes 393224 | tf_op jit(solution)/shard_map/ppermute | solution.py:34
  162.2 8.3 %collective-permute-start.43 = (bf16[1024,128]{0,1:T(8,128)(2,1)S(1)}, bf16[1024,128]{0,1:T(8,128)(2,1)S(1)}, u32[]{:S(2)}, u32[]{:S(2)}) collective-permute-start(bf16[1024,128]{0,1:T(8,128)(2,1)S(1)} %maximum_select_fusion.9), channel_id=1, source_target_pairs={{0,32},{32,0},{8,40},{40,8},{16,48},{48,16},{24,56},{56,24},{64,96... | collective-permute-start | bytes 786440 | tf_op jit(solution)/shard_map/ppermute | solution.py:34
  170.8 4.3 collective-permute-start.44
  170.8 4.3 collective-permute-start.45
  179.4 7.3 %collective-permute-start.49 = (bf16[32,128]{1,0:T(8,128)(2,1)S(1)}, bf16[32,128]{1,0:T(8,128)(2,1)S(1)}, u32[]{:S(2)}, u32[]{:S(2)}) collective-permute-start(bf16[32,128]{1,0:T(8,128)(2,1)S(1)} %collective-permute-done.47), channel_id=1, source_target_pairs={{0,7},{1,0},{2,1},{3,2},{4,3},{5,4},{6,5},{7,6},{8,15},{9,8},{10,9... | collective-permute-start | bytes 24584 | tf_op jit(solution)/shard_map/ppermute | solution.py:20
  188.3 6.9 %collective-permute-start.51 = (bf16[256,128]{0,1:T(8,128)(2,1)S(1)}, bf16[256,128]{0,1:T(8,128)(2,1)S(1)}, u32[]{:S(2)}, u32[]{:S(2)}) collective-permute-start(bf16[256,128]{0,1:T(8,128)(2,1)S(1)} %dynamic_update_slice.191), channel_id=1, source_target_pairs={{0,8},{8,0},{16,24},{24,16},{32,40},{40,32},{48,56},{56,48},{64,72... | collective-permute-start | bytes 196616 | tf_op jit(solution)/shard_map/ppermute | solution.py:34
  195.2 8.4 %collective-permute-start.52 = (bf16[512,128]{0,1:T(8,128)(2,1)S(1)}, bf16[512,128]{0,1:T(8,128)(2,1)S(1)}, u32[]{:S(2)}, u32[]{:S(2)}) collective-permute-start(bf16[512,128]{0,1:T(8,128)(2,1)S(1)} %maximum_select_fusion.18), channel_id=1, source_target_pairs={{0,16},{16,0},{8,24},{24,8},{32,48},{48,32},{40,56},{56,40},{64,80... | collective-permute-start | bytes 393224 | tf_op jit(solution)/shard_map/ppermute | solution.py:34
  203.6 8.4 %collective-permute-start.53 = (bf16[1024,128]{0,1:T(8,128)(2,1)S(1)}, bf16[1024,128]{0,1:T(8,128)(2,1)}, u32[]{:S(2)}, u32[]{:S(2)}) collective-permute-start(bf16[1024,128]{0,1:T(8,128)(2,1)S(1)} %maximum_select_fusion.10), channel_id=1, source_target_pairs={{0,32},{32,0},{8,40},{40,8},{16,48},{48,16},{24,56},{56,24},{64,96... | collective-permute-start | bytes 786440 | tf_op jit(solution)/shard_map/ppermute | solution.py:34
  214.0 11.1 %collective-permute-start.54 = (f32[1024,128]{0,1:T(8,128)S(1)}, f32[1024,128]{0,1:T(8,128)S(1)}, u32[]{:S(2)}, u32[]{:S(2)}) collective-permute-start(f32[1024,128]{0,1:T(8,128)S(1)} %slice_select_fusion.1), channel_id=1, source_target_pairs={{0,32},{32,0},{8,40},{40,8},{16,48},{48,16},{24,56},{56,24},{64,96... | collective-permute-start | bytes 1572872 | tf_op jit(solution)/shard_map/ppermute | solution.py:34
  225.3 9.9 %collective-permute-start.55 = (f32[512,128]{0,1:T(8,128)S(1)}, f32[512,128]{0,1:T(8,128)S(1)}, u32[]{:S(2)}, u32[]{:S(2)}) collective-permute-start(f32[512,128]{0,1:T(8,128)S(1)} %slice_select_fusion.5), channel_id=1, source_target_pairs={{0,16},{16,0},{8,24},{24,8},{32,48},{48,32},{40,56},{56,40},{64,80... | collective-permute-start | bytes 786440 | tf_op jit(solution)/shard_map/ppermute | solution.py:34
  235.2 7.7 %collective-permute-start.56 = (f32[256,128]{0,1:T(8,128)S(1)}, f32[256,128]{0,1:T(8,128)S(1)}, u32[]{:S(2)}, u32[]{:S(2)}) collective-permute-start(f32[256,128]{0,1:T(8,128)S(1)} %slice_select_fusion.11), channel_id=1, source_target_pairs={{0,8},{8,0},{16,24},{24,16},{32,40},{40,32},{48,56},{56,48},{64,72... | collective-permute-start | bytes 393224 | tf_op jit(solution)/shard_map/ppermute | solution.py:34
  243.7 115.5 %reduce-scatter.21.cloned.1.call-start = ((), (), s32[]{:S(2)}) async-start(), calls=%async_computation.7 | async-start | bytes 147456 | tf_op jit(solution)/shard_map/reduce_scatter | solution.py:68
  286.8 13.0 %collective-permute-start.57 = (f32[1024,128]{0,1:T(8,128)S(1)}, f32[1024,128]{0,1:T(8,128)S(1)}, u32[]{:S(2)}, u32[]{:S(2)}) collective-permute-start(f32[1024,128]{0,1:T(8,128)S(1)} %slice_select_fusion), channel_id=1, source_target_pairs={{0,32},{32,0},{8,40},{40,8},{16,48},{48,16},{24,56},{56,24},{64,96... | collective-permute-start | bytes 1572872 | tf_op jit(solution)/shard_map/ppermute | solution.py:34
  299.9 9.8 %collective-permute-start.58 = (f32[512,128]{0,1:T(8,128)S(1)}, f32[512,128]{0,1:T(8,128)S(1)}, u32[]{:S(2)}, u32[]{:S(2)}) collective-permute-start(f32[512,128]{0,1:T(8,128)S(1)} %slice_select_fusion.4), channel_id=1, source_target_pairs={{0,16},{16,0},{8,24},{24,8},{32,48},{48,32},{40,56},{56,40},{64,80... | collective-permute-start | bytes 786440 | tf_op jit(solution)/shard_map/ppermute | solution.py:34
  309.8 6.9 %collective-permute-start.59 = (f32[256,128]{0,1:T(8,128)S(1)}, f32[256,128]{0,1:T(8,128)S(1)}, u32[]{:S(2)}, u32[]{:S(2)}) collective-permute-start(f32[256,128]{0,1:T(8,128)S(1)} %slice_select_fusion.10), channel_id=1, source_target_pairs={{0,8},{8,0},{16,24},{24,16},{32,40},{40,32},{48,56},{56,48},{64,72... | collective-permute-start | bytes 393224 | tf_op jit(solution)/shard_map/ppermute | solution.py:34
  317.5 99.9 %reduce-scatter.23.cloned.1.call-start = ((), (), s32[]{:S(2)}) async-start(), calls=%async_computation.8 | async-start | bytes 147456
  360.4 9.8 %collective-permute-start.60 = (f32[512,128]{0,1:T(8,128)S(1)}, f32[512,128]{0,1:T(8,128)S(1)}, u32[]{:S(2)}, u32[]{:S(2)}) collective-permute-start(f32[512,128]{0,1:T(8,128)S(1)} %slice_select_fusion.3), channel_id=1, source_target_pairs={{0,16},{16,0},{8,24},{24,8},{32,48},{48,32},{40,56},{56,40},{64,80... | collective-permute-start | bytes 786440 | tf_op jit(solution)/shard_map/ppermute | solution.py:34
  370.3 6.9 %collective-permute-start.61 = (f32[256,128]{0,1:T(8,128)S(1)}, f32[256,128]{0,1:T(8,128)S(1)}, u32[]{:S(2)}, u32[]{:S(2)}) collective-permute-start(f32[256,128]{0,1:T(8,128)S(1)} %slice_select_fusion.9), channel_id=1, source_target_pairs={{0,8},{8,0},{16,24},{24,16},{32,40},{40,32},{48,56},{56,48},{64,72... | collective-permute-start | bytes 393224 | tf_op jit(solution)/shard_map/ppermute | solution.py:34
  377.9 97.7 %reduce-scatter.25.cloned.1.call-start = ((), (), s32[]{:S(2)}) async-start(), calls=%async_computation.9 | async-start | bytes 147456 | tf_op jit(solution)/shard_map/reduce_scatter | solution.py:68
  418.5 9.9 %collective-permute-start.62 = (f32[512,128]{0,1:T(8,128)S(1)}, f32[512,128]{0,1:T(8,128)S(1)}, u32[]{:S(2)}, u32[]{:S(2)}) collective-permute-start(f32[512,128]{0,1:T(8,128)S(1)} %slice_select_fusion.2), channel_id=1, source_target_pairs={{0,16},{16,0},{8,24},{24,8},{32,48},{48,32},{40,56},{56,40},{64,80... | collective-permute-start | bytes 786440 | tf_op jit(solution)/shard_map/ppermute | solution.py:34
  428.5 6.9 %collective-permute-start.63 = (f32[256,128]{0,1:T(8,128)S(1)}, f32[256,128]{0,1:T(8,128)S(1)}, u32[]{:S(2)}, u32[]{:S(2)}) collective-permute-start(f32[256,128]{0,1:T(8,128)S(1)} %slice_select_fusion.8), channel_id=1, source_target_pairs={{0,8},{8,0},{16,24},{24,16},{32,40},{40,32},{48,56},{56,48},{64,72... | collective-permute-start | bytes 393224 | tf_op jit(solution)/shard_map/ppermute | solution.py:34
  436.2 85.4 %reduce-scatter.27.cloned.1.call-start = ((), (), s32[]{:S(2)}) async-start(), calls=%async_computation.10 | async-start | bytes 147456
  476.6 6.9 %collective-permute-start.64 = (f32[256,128]{0,1:T(8,128)S(1)}, f32[256,128]{0,1:T(8,128)S(1)}, u32[]{:S(2)}, u32[]{:S(2)}) collective-permute-start(f32[256,128]{0,1:T(8,128)S(1)} %slice_select_fusion.7), channel_id=1, source_target_pairs={{0,8},{8,0},{16,24},{24,16},{32,40},{40,32},{48,56},{56,48},{64,72... | collective-permute-start | bytes 393224 | tf_op jit(solution)/shard_map/ppermute | solution.py:34
  484.3 83.6 %reduce-scatter.29.cloned.1.call-start = ((), (), s32[]{:S(2)}) async-start(), calls=%async_computation.11 | async-start | bytes 147456
  522.6 6.9 %collective-permute-start.65 = (f32[256,128]{0,1:T(8,128)S(1)}, f32[256,128]{0,1:T(8,128)S(1)}, u32[]{:S(2)}, u32[]{:S(2)}) collective-permute-start(f32[256,128]{0,1:T(8,128)S(1)} %slice_select_fusion.6), channel_id=1, source_target_pairs={{0,8},{8,0},{16,24},{24,16},{32,40},{40,32},{48,56},{56,48},{64,72... | collective-permute-start | bytes 393224 | tf_op jit(solution)/shard_map/ppermute | solution.py:34
  (33 other events, 478.2 us)
Sparse Core Ops, SparseCore 0:
  243.9 41.6 reduce-scatter.18
  317.6 41.6 reduce-scatter.20
  378.1 39.2 reduce-scatter.22
  436.3 39.2 reduce-scatter.24
  484.4 37.1 reduce-scatter.26
  530.4 37.4 reduce-scatter.28
